TPU v7x, 128 devices: a whole 4x4x4 slice. The times are simulated.
128 devices in a mesh: gx: 4 (over x), gy: 32 (over z, y, core).
Axes of the slice: x: 4, y: 4, z: 4, core: 2. Of those that a mesh axis runs over, the one named last changes fastest.
Arguments:
- positions: float32 [8192, 3, 128], P(('gx', 'gy')), may hold values from 0 to 64, as said below
- charges: float32 [8192, 128], P(('gx', 'gy')), may hold values from -8 to 8, as said below
- send_x: int32 [128, 2, 32], P(('gx', 'gy')), may hold values from -1 to 63, as said below
- send_y: int32 [128, 2, 32], P(('gx', 'gy')), may hold values from -1 to 63, as said below
- send_corner: int32 [128, 4, 16], P(('gx', 'gy')), may hold values from -1 to 63, as said below
- near_slot: int32 [8192, 27], P(('gx', 'gy')), may hold values from -1 to 255, as said below
- far_sources: int32 [1024, 316], P(('gx', 'gy')), may hold values from -1 to 1023, as said below
- translations: bfloat16 [121, 38236], replicated, may hold values from -0.0078125 to 0.0078125
Outputs:
- potential: float32 [8192, 128], P(('gx', 'gy'))
- field_strength: float32 [8192, 3, 128], P(('gx', 'gy'))
Inputs may be any that keep to these rules, and one draw needn't show every extreme that they name: `send_x`: row [s, k] lists in increasing order, padded with -1, the local indices of the leaves of device s that hold particles and have local x coordinate 0 (k = 0) or 2 - 1 (k = 1); in every draw some device fills both rows. `send_y`: row [s, k] lists in increasing order, padded with -1, the local indices of the leaves of device s that hold particles and have local y coordinate 0 (k = 0) or 2 - 1 (k = 1); in every draw some device fills both rows. `send_corner`: row [s, k], k = 2 kx + ky, lists in increasing order, padded with -1, the local indices of the leaves of device s that hold particles and have local x coordinate kx (1) and local y coordinate ky (1); in every draw some device fills all four rows. `near_slot`: offset n = 9 (a + 1) + 3 (b + 1) + (c + 1) for the neighbour at (a, b, c) in -1..1; -1 where that leaf lies outside the domain or holds no particles; otherwise the entry of the owner's source table that holds it (n = 13 is the leaf itself). `far_sources`: class k is the k-th offset (a, b, c) in -3..3 with max(|a|, |b|, |c|) > 1, taken in increasing 49 a + 7 b + c; the entry is the upper cell at that offset where it lies in the domain, holds particles and its parent (coordinates halved, rounded down) touches or equals the parent of m, else -1. positions[g, :, p] lies in the unit box of leaf g. `charges`: empty leaves and the slots after each leaf's particle count hold zero.
All inputs are finite; a program needn't handle non-finite values.
Results may differ from a plain program's by a relative error of at most 0.0003.
Values may be sent and summed in bfloat16 or wider, within the bound.
A program may use at most 64 MiB of HBM per device.

v0:
```python
import math
import jax
import jax.numpy as jnp
from jax import lax
from jax.sharding import PartitionSpec as P

ORDER = 10
COEF = 121
BX = 2
BY = 2
BZ = 16
UP_DEV = 8
softening = 0.01


def passed_along(value, axis, steps):
    count = lax.axis_size(axis)
    first, last = (max(0, -steps), min(count, count - steps))
    return lax.ppermute(value, axis, [(source, source + steps) for source in range(first, last)])


def upper_centers(cells, row_count):
    half_y = BY // 2
    half_z = BZ // 2
    device = cells // UP_DEV
    local_ids = cells % UP_DEV
    cell_x = device // row_count * (BX // 2) + local_ids // (half_y * half_z)
    cell_y = device % row_count * half_y + local_ids // half_z % half_y
    cell_z = local_ids % half_z
    return 2.0 * jnp.stack([cell_x, cell_y, cell_z], axis=1).astype(jnp.float32) + 1.0


def harmonics(xcoord, ycoord, zcoord):
    radius_sq = xcoord * xcoord + ycoord * ycoord + zcoord * zcoord
    unity = jnp.ones_like(xcoord)
    nothing = jnp.zeros_like(xcoord)
    solid_harm = {(0, 0): (unity, nothing)}
    for moment in range(1, ORDER + 1):
        real_part, imag_part = solid_harm[moment - 1, moment - 1]
        factor = -0.5 / moment
        solid_harm[moment, moment] = (
            factor * (xcoord * real_part - ycoord * imag_part),
            factor * (xcoord * imag_part + ycoord * real_part),
        )
    for moment in range(ORDER + 1):
        if moment + 1 <= ORDER:
            real_part, imag_part = solid_harm[moment, moment]
            solid_harm[moment + 1, moment] = (zcoord * real_part, zcoord * imag_part)
        for degree in range(moment + 2, ORDER + 1):
            factor = 1.0 / ((degree - moment) * (degree + moment))
            one_back = solid_harm[degree - 1, moment]
            two_back = solid_harm[degree - 2, moment]
            solid_harm[degree, moment] = (
                factor * ((2 * degree - 1) * zcoord * one_back[0] - radius_sq * two_back[0]),
                factor * ((2 * degree - 1) * zcoord * one_back[1] - radius_sq * two_back[1]),
            )
    stacked = []
    for degree in range(ORDER + 1):
        for moment in range(degree + 1):
            scaling = math.sqrt(math.factorial(degree + moment) * math.factorial(degree - moment))
            real_part, imag_part = solid_harm[degree, moment]
            stacked.append(scaling * real_part)
            if moment > 0:
                stacked.append(scaling * imag_part)
    return jnp.stack(stacked, axis=0)


def leaf_multipoles(positions, charges, centers):
    repeated = jnp.repeat(centers, 8, axis=0)
    offsets = positions - repeated[:, :, None]
    harm = harmonics(offsets[:, 0], offsets[:, 1], offsets[:, 2])
    per_leaf = jnp.sum(harm * charges[None], axis=2)
    return per_leaf.reshape(COEF, -1, 8).sum(axis=2)


def far_field(positions, centers, local_exp):
    repeated = jnp.repeat(centers, 8, axis=0)
    per_leaf = jnp.repeat(local_exp, 8, axis=1)

    def summed_field(points):
        offsets = points - repeated[:, :, None]
        harm = harmonics(offsets[:, 0], offsets[:, 1], offsets[:, 2])
        return jnp.sum(harm * per_leaf[:, :, None], axis=0)

    potential, pullback = jax.vjp(summed_field, positions)
    gradient = pullback(jnp.ones_like(potential))[0]
    return (potential, -gradient)


def translate(everyone, far_sources, translations):
    usable = far_sources >= 0
    picked = jnp.take(everyone, jnp.maximum(far_sources, 0), axis=1)
    picked = jnp.where(usable[None], picked, jnp.zeros((), picked.dtype))
    stacked = jnp.transpose(picked, (1, 2, 0)).reshape(picked.shape[1], -1)
    return jnp.einsum("uk,ik->iu", stacked, translations, preferred_element_type=jnp.float32)


def near_field(targets, source_points, source_charge, slot_ids):
    identity = jnp.eye(targets.shape[2], dtype=jnp.float32)

    def neighbour_step(running, inputs):
        potential, electric = running
        column, neighbour = inputs
        present = column >= 0
        safe = jnp.maximum(column, 0)
        points = source_points[safe]
        charge = jnp.where(present[:, None], source_charge[safe], 0.0)
        separation = targets[:, :, :, None] - points[:, :, None, :]
        distance = jnp.sum(separation * separation, axis=1) + softening
        inverse = lax.rsqrt(distance)
        self_mask = jnp.where(neighbour == 13, 1.0 - identity, 1.0)
        weight = charge[:, None, :] * inverse * self_mask
        potential = potential + jnp.sum(weight, axis=2)
        electric = electric + jnp.sum(separation * (weight * inverse * inverse)[:, None], axis=3)
        return ((potential, electric), None)

    start = (
        jnp.zeros(targets.shape[:1] + targets.shape[2:], jnp.float32),
        jnp.zeros(targets.shape, jnp.float32),
    )
    result = lax.scan(neighbour_step, start, (slot_ids.T, jnp.arange(27, dtype=jnp.int32)))[0]
    return result


def pack_blocks(listing, positions, charges):
    present = listing >= 0
    chosen = jnp.maximum(listing, 0)
    points = jnp.where(present[:, :, None, None], positions[chosen], 0.0)
    charge = jnp.where(present[:, :, None], charges[chosen], 0.0)
    return jnp.concatenate([points, charge[:, :, None]], axis=2)


def per_device(
    positions, charges, send_x, send_y, send_corner, near_slot, far_sources, translations
):
    inner_count = lax.axis_size("gy")
    device = lax.axis_index("gx") * inner_count + lax.axis_index("gy")
    cells = device * UP_DEV + jnp.arange(UP_DEV, dtype=jnp.int32)
    centers = upper_centers(cells, inner_count)
    multipole = leaf_multipoles(positions, charges, centers).astype(jnp.bfloat16)
    everyone = lax.all_gather(multipole, ("gx", "gy"), axis=1, tiled=True)
    local_exp = translate(everyone, far_sources, translations)
    far_pot, far_force = far_field(positions, centers, local_exp)
    own_blocks = jnp.concatenate([positions, charges[:, None]], axis=1)
    packed_x = pack_blocks(send_x[0], positions, charges)
    packed_y = pack_blocks(send_y[0], positions, charges)
    packed_edge = pack_blocks(send_corner[0], positions, charges)
    table_parts = [own_blocks]
    for block in range(2):
        table_parts.append(passed_along(packed_x[1 - block], "gx", 1 - 2 * block))
    for block in range(2):
        table_parts.append(passed_along(packed_y[1 - block], "gy", 1 - 2 * block))
    for block in range(4):
        step_x = 2 * (block // 2) - 1
        step_y = 2 * (block % 2) - 1
        table_parts.append(
            passed_along(packed_edge[3 - block], ("gx", "gy"), -(step_x * inner_count + step_y))
        )
    table = jnp.concatenate(table_parts, axis=0)
    near_pot, near_force = near_field(positions, table[:, :3], table[:, 3], near_slot)
    return (far_pot + near_pot, far_force + near_force)


def solution(mesh):
    return jax.shard_map(
        per_device,
        mesh=mesh,
        in_specs=(
            P(("gx", "gy"), None, None),
            P(("gx", "gy"), None),
            P(("gx", "gy"), None, None),
            P(("gx", "gy"), None, None),
            P(("gx", "gy"), None, None),
            P(("gx", "gy"), None),
            P(("gx", "gy"), None),
            P(),
        ),
        out_specs=(P(("gx", "gy"), None), P(("gx", "gy"), None, None)),
        check_vma=False,
    )
```

profile of v0, /device:TPU:121, one launch (start us, length us, event | category | flops | bytes accessed | tf_op | source)
XLA Modules:
  0.0 867.6 jit_solution(16908647988988412900)
XLA Ops:
  105.4 37.0 %all_gather.3 = bf16[121,1024]{0,1:T(8,128)(2,1)S(1)} all-gather(bf16[121,8]{0,1:T(8,128)(2,1)S(1)} %bitcast_reduce_fusion), channel_id=1, replica_groups=mesh['gx'=4,'gy'=32] {'gx','gy'}, dimensions={1}, use_global_device_ids=true | all-gather | bytes 249744 | tf_op jit(solution)/shard_map/all_gather | solution.py:141
  193.6 6.3 collective-permute-start.6
  202.2 8.8 %collective-permute-done.7 = f32[16,4,128]{2,1,0:T(4,128)S(1)} collective-permute-done((f32[16,4,128]{2,1,0:T(4,128)S(1)}, f32[16,4,128]{2,1,0:T(4,128)S(1)}, u32[]{:S(2)}, u32[]{:S(2)}) %collective-permute-start.7) | collective-permute-done | bytes 32800 | tf_op jit(solution)/shard_map/ppermute | solution.py:19
  211.1 655.2 %while.13 = (s32[]{:T(128)}, f32[64,128]{1,0:T(8,128)S(1)}, f32[64,3,128]{2,1,0:T(4,128)S(1)}, s32[27,64]{1,0:T(8,128)}, f32[256,128]{1,0:T(8,128)S(1)}, /*index...) while((s32[]{:T(128)}, f32[64,128]{1,0:T(8,128)S(1)}, ...), condition=%wide.region_7.8_spmd.clone, body=%wide.region_3.7_spmd.clone.sunk | while | flops 24224900 | bytes 18192156 | solution.py:121
  212.5 6.0 fusion.453
  226.4 8.9 %fusion.455 = f32[64,3,128]{2,1,0:T(4,128)S(1)} fusion(f32[64,128,128]{2,1,0:T(8,128)} %get-tuple-element.385, f32[64,3,128]{2,1,0:T(4,128)S(1)} %gather_fusion, f32[64,3,128]{2,1,0:T(4,128)S(1)} %get-tuple-element.413), kind=kLoop, calls=%fused_computation.13.clone.1 | loop fusion | flops 9412608 | bytes 4489216 | tf_op jit(solution)/shard_map/while/body/eval_jaxpr/reduce_sum | solution.py:114
  236.8 6.0 fusion.453
  250.6 8.9 %fusion.455 = f32[64,3,128]{2,1,0:T(4,128)S(1)} fusion(f32[64,128,128]{2,1,0:T(8,128)} %get-tuple-element.385, f32[64,3,128]{2,1,0:T(4,128)S(1)} %gather_fusion, f32[64,3,128]{2,1,0:T(4,128)S(1)} %get-tuple-element.413), kind=kLoop, calls=%fused_computation.13.clone.1 | loop fusion | flops 9412608 | bytes 4489216 | tf_op jit(solution)/shard_map/while/body/eval_jaxpr/reduce_sum | solution.py:114
  261.0 6.0 fusion.453
  274.9 8.9 %fusion.455 = f32[64,3,128]{2,1,0:T(4,128)S(1)} fusion(f32[64,128,128]{2,1,0:T(8,128)} %get-tuple-element.385, f32[64,3,128]{2,1,0:T(4,128)S(1)} %gather_fusion, f32[64,3,128]{2,1,0:T(4,128)S(1)} %get-tuple-element.413), kind=kLoop, calls=%fused_computation.13.clone.1 | loop fusion | flops 9412608 | bytes 4489216 | tf_op jit(solution)/shard_map/while/body/eval_jaxpr/reduce_sum | solution.py:114
  285.3 6.0 fusion.453
  299.2 8.9 %fusion.455 = f32[64,3,128]{2,1,0:T(4,128)S(1)} fusion(f32[64,128,128]{2,1,0:T(8,128)} %get-tuple-element.385, f32[64,3,128]{2,1,0:T(4,128)S(1)} %gather_fusion, f32[64,3,128]{2,1,0:T(4,128)S(1)} %get-tuple-element.413), kind=kLoop, calls=%fused_computation.13.clone.1 | loop fusion | flops 9412608 | bytes 4489216 | tf_op jit(solution)/shard_map/while/body/eval_jaxpr/reduce_sum | solution.py:114
  309.6 6.0 fusion.453
  323.4 8.9 %fusion.455 = f32[64,3,128]{2,1,0:T(4,128)S(1)} fusion(f32[64,128,128]{2,1,0:T(8,128)} %get-tuple-element.385, f32[64,3,128]{2,1,0:T(4,128)S(1)} %gather_fusion, f32[64,3,128]{2,1,0:T(4,128)S(1)} %get-tuple-element.413), kind=kLoop, calls=%fused_computation.13.clone.1 | loop fusion | flops 9412608 | bytes 4489216 | tf_op jit(solution)/shard_map/while/body/eval_jaxpr/reduce_sum | solution.py:114
  333.8 6.0 fusion.453
  347.7 8.9 %fusion.455 = f32[64,3,128]{2,1,0:T(4,128)S(1)} fusion(f32[64,128,128]{2,1,0:T(8,128)} %get-tuple-element.385, f32[64,3,128]{2,1,0:T(4,128)S(1)} %gather_fusion, f32[64,3,128]{2,1,0:T(4,128)S(1)} %get-tuple-element.413), kind=kLoop, calls=%fused_computation.13.clone.1 | loop fusion | flops 9412608 | bytes 4489216 | tf_op jit(solution)/shard_map/while/body/eval_jaxpr/reduce_sum | solution.py:114
  358.1 6.0 fusion.453
  372.0 8.9 %fusion.455 = f32[64,3,128]{2,1,0:T(4,128)S(1)} fusion(f32[64,128,128]{2,1,0:T(8,128)} %get-tuple-element.385, f32[64,3,128]{2,1,0:T(4,128)S(1)} %gather_fusion, f32[64,3,128]{2,1,0:T(4,128)S(1)} %get-tuple-element.413), kind=kLoop, calls=%fused_computation.13.clone.1 | loop fusion | flops 9412608 | bytes 4489216 | tf_op jit(solution)/shard_map/while/body/eval_jaxpr/reduce_sum | solution.py:114
  396.2 8.9 %fusion.455 = f32[64,3,128]{2,1,0:T(4,128)S(1)} fusion(f32[64,128,128]{2,1,0:T(8,128)} %get-tuple-element.385, f32[64,3,128]{2,1,0:T(4,128)S(1)} %gather_fusion, f32[64,3,128]{2,1,0:T(4,128)S(1)} %get-tuple-element.413), kind=kLoop, calls=%fused_computation.13.clone.1 | loop fusion | flops 9412608 | bytes 4489216 | tf_op jit(solution)/shard_map/while/body/eval_jaxpr/reduce_sum | solution.py:114
  406.6 6.0 fusion.453
  420.5 8.9 %fusion.455 = f32[64,3,128]{2,1,0:T(4,128)S(1)} fusion(f32[64,128,128]{2,1,0:T(8,128)} %get-tuple-element.385, f32[64,3,128]{2,1,0:T(4,128)S(1)} %gather_fusion, f32[64,3,128]{2,1,0:T(4,128)S(1)} %get-tuple-element.413), kind=kLoop, calls=%fused_computation.13.clone.1 | loop fusion | flops 9412608 | bytes 4489216 | tf_op jit(solution)/shard_map/while/body/eval_jaxpr/reduce_sum | solution.py:114
  430.9 6.0 fusion.453
  444.8 8.9 %fusion.455 = f32[64,3,128]{2,1,0:T(4,128)S(1)} fusion(f32[64,128,128]{2,1,0:T(8,128)} %get-tuple-element.385, f32[64,3,128]{2,1,0:T(4,128)S(1)} %gather_fusion, f32[64,3,128]{2,1,0:T(4,128)S(1)} %get-tuple-element.413), kind=kLoop, calls=%fused_computation.13.clone.1 | loop fusion | flops 9412608 | bytes 4489216 | tf_op jit(solution)/shard_map/while/body/eval_jaxpr/reduce_sum | solution.py:114
  455.2 6.0 fusion.453
  469.0 8.9 %fusion.455 = f32[64,3,128]{2,1,0:T(4,128)S(1)} fusion(f32[64,128,128]{2,1,0:T(8,128)} %get-tuple-element.385, f32[64,3,128]{2,1,0:T(4,128)S(1)} %gather_fusion, f32[64,3,128]{2,1,0:T(4,128)S(1)} %get-tuple-element.413), kind=kLoop, calls=%fused_computation.13.clone.1 | loop fusion | flops 9412608 | bytes 4489216 | tf_op jit(solution)/shard_map/while/body/eval_jaxpr/reduce_sum | solution.py:114
  479.4 6.0 fusion.453
  493.3 8.9 %fusion.455 = f32[64,3,128]{2,1,0:T(4,128)S(1)} fusion(f32[64,128,128]{2,1,0:T(8,128)} %get-tuple-element.385, f32[64,3,128]{2,1,0:T(4,128)S(1)} %gather_fusion, f32[64,3,128]{2,1,0:T(4,128)S(1)} %get-tuple-element.413), kind=kLoop, calls=%fused_computation.13.clone.1 | loop fusion | flops 9412608 | bytes 4489216 | tf_op jit(solution)/shard_map/while/body/eval_jaxpr/reduce_sum | solution.py:114
  503.7 6.0 fusion.453
  517.6 8.9 %fusion.455 = f32[64,3,128]{2,1,0:T(4,128)S(1)} fusion(f32[64,128,128]{2,1,0:T(8,128)} %get-tuple-element.385, f32[64,3,128]{2,1,0:T(4,128)S(1)} %gather_fusion, f32[64,3,128]{2,1,0:T(4,128)S(1)} %get-tuple-element.413), kind=kLoop, calls=%fused_computation.13.clone.1 | loop fusion | flops 9412608 | bytes 4489216 | tf_op jit(solution)/shard_map/while/body/eval_jaxpr/reduce_sum | solution.py:114
  541.8 8.9 %fusion.455 = f32[64,3,128]{2,1,0:T(4,128)S(1)} fusion(f32[64,128,128]{2,1,0:T(8,128)} %get-tuple-element.385, f32[64,3,128]{2,1,0:T(4,128)S(1)} %gather_fusion, f32[64,3,128]{2,1,0:T(4,128)S(1)} %get-tuple-element.413), kind=kLoop, calls=%fused_computation.13.clone.1 | loop fusion | flops 9412608 | bytes 4489216 | tf_op jit(solution)/shard_map/while/body/eval_jaxpr/reduce_sum | solution.py:114
  552.2 6.0 fusion.453
  566.1 8.9 %fusion.455 = f32[64,3,128]{2,1,0:T(4,128)S(1)} fusion(f32[64,128,128]{2,1,0:T(8,128)} %get-tuple-element.385, f32[64,3,128]{2,1,0:T(4,128)S(1)} %gather_fusion, f32[64,3,128]{2,1,0:T(4,128)S(1)} %get-tuple-element.413), kind=kLoop, calls=%fused_computation.13.clone.1 | loop fusion | flops 9412608 | bytes 4489216 | tf_op jit(solution)/shard_map/while/body/eval_jaxpr/reduce_sum | solution.py:114
  590.4 8.9 %fusion.455 = f32[64,3,128]{2,1,0:T(4,128)S(1)} fusion(f32[64,128,128]{2,1,0:T(8,128)} %get-tuple-element.385, f32[64,3,128]{2,1,0:T(4,128)S(1)} %gather_fusion, f32[64,3,128]{2,1,0:T(4,128)S(1)} %get-tuple-element.413), kind=kLoop, calls=%fused_computation.13.clone.1 | loop fusion | flops 9412608 | bytes 4489216 | tf_op jit(solution)/shard_map/while/body/eval_jaxpr/reduce_sum | solution.py:114
  614.6 8.9 %fusion.455 = f32[64,3,128]{2,1,0:T(4,128)S(1)} fusion(f32[64,128,128]{2,1,0:T(8,128)} %get-tuple-element.385, f32[64,3,128]{2,1,0:T(4,128)S(1)} %gather_fusion, f32[64,3,128]{2,1,0:T(4,128)S(1)} %get-tuple-element.413), kind=kLoop, calls=%fused_computation.13.clone.1 | loop fusion | flops 9412608 | bytes 4489216 | tf_op jit(solution)/shard_map/while/body/eval_jaxpr/reduce_sum | solution.py:114
  638.9 8.9 %fusion.455 = f32[64,3,128]{2,1,0:T(4,128)S(1)} fusion(f32[64,128,128]{2,1,0:T(8,128)} %get-tuple-element.385, f32[64,3,128]{2,1,0:T(4,128)S(1)} %gather_fusion, f32[64,3,128]{2,1,0:T(4,128)S(1)} %get-tuple-element.413), kind=kLoop, calls=%fused_computation.13.clone.1 | loop fusion | flops 9412608 | bytes 4489216 | tf_op jit(solution)/shard_map/while/body/eval_jaxpr/reduce_sum | solution.py:114
  649.3 6.0 fusion.453
  663.2 8.9 %fusion.455 = f32[64,3,128]{2,1,0:T(4,128)S(1)} fusion(f32[64,128,128]{2,1,0:T(8,128)} %get-tuple-element.385, f32[64,3,128]{2,1,0:T(4,128)S(1)} %gather_fusion, f32[64,3,128]{2,1,0:T(4,128)S(1)} %get-tuple-element.413), kind=kLoop, calls=%fused_computation.13.clone.1 | loop fusion | flops 9412608 | bytes 4489216 | tf_op jit(solution)/shard_map/while/body/eval_jaxpr/reduce_sum | solution.py:114
  673.6 6.0 fusion.453
  687.4 8.9 %fusion.455 = f32[64,3,128]{2,1,0:T(4,128)S(1)} fusion(f32[64,128,128]{2,1,0:T(8,128)} %get-tuple-element.385, f32[64,3,128]{2,1,0:T(4,128)S(1)} %gather_fusion, f32[64,3,128]{2,1,0:T(4,128)S(1)} %get-tuple-element.413), kind=kLoop, calls=%fused_computation.13.clone.1 | loop fusion | flops 9412608 | bytes 4489216 | tf_op jit(solution)/shard_map/while/body/eval_jaxpr/reduce_sum | solution.py:114
  711.7 8.9 %fusion.455 = f32[64,3,128]{2,1,0:T(4,128)S(1)} fusion(f32[64,128,128]{2,1,0:T(8,128)} %get-tuple-element.385, f32[64,3,128]{2,1,0:T(4,128)S(1)} %gather_fusion, f32[64,3,128]{2,1,0:T(4,128)S(1)} %get-tuple-element.413), kind=kLoop, calls=%fused_computation.13.clone.1 | loop fusion | flops 9412608 | bytes 4489216 | tf_op jit(solution)/shard_map/while/body/eval_jaxpr/reduce_sum | solution.py:114
  722.1 6.0 fusion.453
  736.0 8.9 %fusion.455 = f32[64,3,128]{2,1,0:T(4,128)S(1)} fusion(f32[64,128,128]{2,1,0:T(8,128)} %get-tuple-element.385, f32[64,3,128]{2,1,0:T(4,128)S(1)} %gather_fusion, f32[64,3,128]{2,1,0:T(4,128)S(1)} %get-tuple-element.413), kind=kLoop, calls=%fused_computation.13.clone.1 | loop fusion | flops 9412608 | bytes 4489216 | tf_op jit(solution)/shard_map/while/body/eval_jaxpr/reduce_sum | solution.py:114
  746.4 6.0 fusion.453
  760.2 8.9 %fusion.455 = f32[64,3,128]{2,1,0:T(4,128)S(1)} fusion(f32[64,128,128]{2,1,0:T(8,128)} %get-tuple-element.385, f32[64,3,128]{2,1,0:T(4,128)S(1)} %gather_fusion, f32[64,3,128]{2,1,0:T(4,128)S(1)} %get-tuple-element.413), kind=kLoop, calls=%fused_computation.13.clone.1 | loop fusion | flops 9412608 | bytes 4489216 | tf_op jit(solution)/shard_map/while/body/eval_jaxpr/reduce_sum | solution.py:114
  784.5 8.9 %fusion.455 = f32[64,3,128]{2,1,0:T(4,128)S(1)} fusion(f32[64,128,128]{2,1,0:T(8,128)} %get-tuple-element.385, f32[64,3,128]{2,1,0:T(4,128)S(1)} %gather_fusion, f32[64,3,128]{2,1,0:T(4,128)S(1)} %get-tuple-element.413), kind=kLoop, calls=%fused_computation.13.clone.1 | loop fusion | flops 9412608 | bytes 4489216 | tf_op jit(solution)/shard_map/while/body/eval_jaxpr/reduce_sum | solution.py:114
  808.8 8.9 %fusion.455 = f32[64,3,128]{2,1,0:T(4,128)S(1)} fusion(f32[64,128,128]{2,1,0:T(8,128)} %get-tuple-element.385, f32[64,3,128]{2,1,0:T(4,128)S(1)} %gather_fusion, f32[64,3,128]{2,1,0:T(4,128)S(1)} %get-tuple-element.413), kind=kLoop, calls=%fused_computation.13.clone.1 | loop fusion | flops 9412608 | bytes 4489216 | tf_op jit(solution)/shard_map/while/body/eval_jaxpr/reduce_sum | solution.py:114
  833.0 8.9 %fusion.455 = f32[64,3,128]{2,1,0:T(4,128)S(1)} fusion(f32[64,128,128]{2,1,0:T(8,128)} %get-tuple-element.385, f32[64,3,128]{2,1,0:T(4,128)S(1)} %gather_fusion, f32[64,3,128]{2,1,0:T(4,128)S(1)} %get-tuple-element.413), kind=kLoop, calls=%fused_computation.13.clone.1 | loop fusion | flops 9412608 | bytes 4489216 | tf_op jit(solution)/shard_map/while/body/eval_jaxpr/reduce_sum | solution.py:114
  857.3 8.9 %fusion.455 = f32[64,3,128]{2,1,0:T(4,128)S(1)} fusion(f32[64,128,128]{2,1,0:T(8,128)} %get-tuple-element.385, f32[64,3,128]{2,1,0:T(4,128)S(1)} %gather_fusion, f32[64,3,128]{2,1,0:T(4,128)S(1)} %get-tuple-element.413), kind=kLoop, calls=%fused_computation.13.clone.1 | loop fusion | flops 9412608 | bytes 4489216 | tf_op jit(solution)/shard_map/while/body/eval_jaxpr/reduce_sum | solution.py:114
  (856 shorter events, 453.5 us)
Async XLA Ops:
  0.6 19.6 %copy-start.1 = (f32[64,128]{1,0:T(8,128)S(1)}, f32[64,128]{1,0:T(8,128)}, u32[]{:S(2)}) copy-start(f32[64,128]{1,0:T(8,128)} %param.11) | copy-start | bytes 98308
  0.6 20.2 %copy-start = (f32[64,3,128]{2,0,1:T(8,128)S(1)}, f32[64,3,128]{2,0,1:T(8,128)}, u32[]{:S(2)}) copy-start(f32[64,3,128]{2,0,1:T(8,128)} %param.10) | copy-start | bytes 294916
  0.7 19.6 %copy-start.5 = (s32[1,4,16]{2,1,0:T(4,128)S(1)}, s32[1,4,16]{2,1,0:T(4,128)}, u32[]{:S(2)}) copy-start(s32[1,4,16]{2,1,0:T(4,128)} %param.14) | copy-start | bytes 772
  0.7 25.9 %copy-start.2 = (s32[8,316]{1,0:T(8,128)S(1)}, s32[8,316]{1,0:T(8,128)}, u32[]{:S(2)}) copy-start(s32[8,316]{1,0:T(8,128)} %param.16) | copy-start | bytes 30340
  5.5 185.5 %collective-permute-start = (f32[32,4,128]{2,1,0:T(4,128)S(1)}, f32[32,4,128]{2,1,0:T(4,128)S(1)}, u32[]{:S(2)}, u32[]{:S(2)}) collective-permute-start(f32[32,4,128]{2,1,0:T(4,128)S(1)} %get-tuple-element.310), channel_id=1, source_target_pairs={{0,32},{32,64},{64,96},{1,33},{33,65},{65,97},{2,34},{34,66},{66,9... | collective-permute-start | bytes 196616 | tf_op jit(solution)/shard_map/ppermute | solution.py:19
  8.6 185.0 %collective-permute-start.1 = (f32[32,4,128]{2,1,0:T(4,128)S(1)}, f32[32,4,128]{2,1,0:T(4,128)S(1)}, u32[]{:S(2)}, u32[]{:S(2)}) collective-permute-start(f32[32,4,128]{2,1,0:T(4,128)S(1)} %get-tuple-element.309), channel_id=1, source_target_pairs={{32,0},{64,32},{96,64},{33,1},{65,33},{97,65},{34,2},{66,34},{98,6... | collective-permute-start | bytes 196616 | tf_op jit(solution)/shard_map/ppermute | solution.py:19
  15.4 184.6 %collective-permute-start.2 = (f32[32,4,128]{2,1,0:T(4,128)S(1)}, f32[32,4,128]{2,1,0:T(4,128)S(1)}, u32[]{:S(2)}, u32[]{:S(2)}) collective-permute-start(f32[32,4,128]{2,1,0:T(4,128)S(1)} %get-tuple-element.308), channel_id=1, source_target_pairs={{0,1},{1,2},{2,3},{3,4},{4,5},{5,6},{6,7},{7,8},{8,9},{9,10},{10,1... | collective-permute-start | bytes 196616 | tf_op jit(solution)/shard_map/ppermute | solution.py:19
  16.7 184.6 %collective-permute-start.3 = (f32[32,4,128]{2,1,0:T(4,128)S(1)}, f32[32,4,128]{2,1,0:T(4,128)S(1)}, u32[]{:S(2)}, u32[]{:S(2)}) collective-permute-start(f32[32,4,128]{2,1,0:T(4,128)S(1)} %get-tuple-element.307), channel_id=1, source_target_pairs={{1,0},{2,1},{3,2},{4,3},{5,4},{6,5},{7,6},{8,7},{9,8},{10,9},{11,1... | collective-permute-start | bytes 196616 | tf_op jit(solution)/shard_map/ppermute | solution.py:19
  22.5 178.8 %collective-permute-start.4 = (f32[16,4,128]{2,1,0:T(4,128)}, f32[16,4,128]{2,1,0:T(4,128)}, u32[]{:S(2)}, u32[]{:S(2)}) collective-permute-start(f32[16,4,128]{2,1,0:T(4,128)} %get-tuple-element.304), channel_id=1, source_target_pairs={{0,33},{1,34},{2,35},{3,36},{4,37},{5,38},{6,39},{7,40},{8,41},{9,... | collective-permute-start | bytes 98312 | tf_op jit(solution)/shard_map/ppermute | solution.py:19
  154.4 36.6 %copy-start.4 = (f32[16,4,128]{2,1,0:T(4,128)S(1)}, f32[16,4,128]{2,1,0:T(4,128)}, u32[]{:S(2)}) copy-start(f32[16,4,128]{2,1,0:T(4,128)} %get-tuple-element.305) | copy-start | bytes 98308
  154.9 38.7 %copy-start.3 = (f32[16,4,128]{2,1,0:T(4,128)S(1)}, f32[16,4,128]{2,1,0:T(4,128)}, u32[]{:S(2)}) copy-start(f32[16,4,128]{2,1,0:T(4,128)} %get-tuple-element.306) | copy-start | bytes 98308
  191.0 11.1 %collective-permute-start.5 = (f32[16,4,128]{2,1,0:T(4,128)S(1)}, f32[16,4,128]{2,1,0:T(4,128)S(1)}, u32[]{:S(2)}, u32[]{:S(2)}) collective-permute-start(f32[16,4,128]{2,1,0:T(4,128)S(1)} %copy-done.4), channel_id=1, source_target_pairs={{0,31},{1,32},{2,33},{3,34},{4,35},{5,36},{6,37},{7,38},{8,39},{9,... | collective-permute-start | bytes 98312 | tf_op jit(solution)/shard_map/ppermute | solution.py:19
  193.6 8.5 collective-permute-start.6
  200.0 11.0 %collective-permute-start.7 = (f32[16,4,128]{2,1,0:T(4,128)S(1)}, f32[16,4,128]{2,1,0:T(4,128)S(1)}, u32[]{:S(2)}, u32[]{:S(2)}) collective-permute-start(f32[16,4,128]{2,1,0:T(4,128)S(1)} %get-tuple-element.303), channel_id=1, source_target_pairs={{33,0},{34,1},{35,2},{36,3},{37,4},{38,5},{39,6},{40,7},{41,8},{42... | collective-permute-start | bytes 98312 | tf_op jit(solution)/shard_map/ppermute | solution.py:19
where the time goes:
time: 875 us; the launch traced here: 868 us
  other arithmetic  685 us (78%)
  local copies, waits for them, and re-layouts  89.5 us (10%)
  blocking collectives  37 us (4%)
  starting transfers between devices  22.7 us (3%)
  loops' own time  18.4 us (2%)
  waiting for transfers between devices  8.81 us (1%)
    reduce_sum x27, other arithmetic, neighbour_step(): jnp.sum(separation * (weight * inverse * inverse)[:, None], axis=3)  239 us
    reduce_sum x27, other arithmetic, neighbour_step(): distance = jnp.sum(separation * separation, axis=1) + softening  163 us
    mul x27, other arithmetic, neighbour_step(): weight * inverse * inverse  140 us
    unnamed x121, other arithmetic  73.9 us
    all_gather x1, blocking collectives, per_device(): everyone = lax.all_gather(multipole, ('gx', 'gy'), axis=1, tiled=True)  37 us
    ppermute x8, starting transfers between devices, passed_along(): lax.ppermute(value, axis, [(source, source + steps) for source in range(f...  22.7 us
    max x27, other arithmetic, neighbour_step(): safe = jnp.maximum(column, 0)  18.8 us
    ge x27, other arithmetic, neighbour_step(): present = column >= 0  18.8 us
  transfers between devices with their start and end apart: 8, of which 1 were waited for; matrix products, arithmetic and copies ran while one was open for 16% of the time, Pallas kernels for 0%

commit v1 on v0

--- a/solution.py
+++ b/solution.py
@@ -138,7 +138,10 @@
     cells = device * UP_DEV + jnp.arange(UP_DEV, dtype=jnp.int32)
     centers = upper_centers(cells, inner_count)
     multipole = leaf_multipoles(positions, charges, centers).astype(jnp.bfloat16)
-    everyone = lax.all_gather(multipole, ("gx", "gy"), axis=1, tiled=True)
+    everyone = jnp.concatenate(
+        lax.all_to_all(jnp.stack([multipole] * lax.axis_size(("gx", "gy"))), ("gx", "gy"), 0, 0),
+        axis=1,
+    )
     local_exp = translate(everyone, far_sources, translations)
     far_pot, far_force = far_field(positions, centers, local_exp)
     own_blocks = jnp.concatenate([positions, charges[:, None]], axis=1)

time: 875 us -> 845 us (0.966)
  blocking collectives: 37 us -> 0 us
  starting transfers between devices: 22.7 us -> 33 us
    all_gather x1 -> x0, blocking collectives: 37 us -> none  [per_device(): everyone = lax.all_gather(multipole, ('gx', 'gy'), axis=1, tiled=True)]
    all_to_all x0 -> x1, starting transfers between devices: none -> 10 us  [per_device(): lax.all_to_all(jnp.stack([multipole] * lax.axis_size(('gx', 'gy'))), ('gx...]
  transfers between devices with their start and end apart: 8 -> 9, of which waited for: 1 -> 2; matrix products, arithmetic and copies ran while one was open for 16% -> 77% of each run, Pallas kernels for 0% -> 0%
where the time goes in v1:
time: 845 us; the launch traced here: 835 us
  other arithmetic  681 us (81%)
  local copies, waits for them, and re-layouts  86.2 us (10%)
  starting transfers between devices  33 us (4%)
  loops' own time  18.4 us (2%)
  waiting for transfers between devices  9.38 us (1%)
    reduce_sum x27, other arithmetic, neighbour_step(): jnp.sum(separation * (weight * inverse * inverse)[:, None], axis=3)  239 us
    reduce_sum x27, other arithmetic, neighbour_step(): distance = jnp.sum(separation * separation, axis=1) + softening  163 us
    mul x27, other arithmetic, neighbour_step(): weight * inverse * inverse  140 us
    unnamed x121, other arithmetic  73.9 us
    ppermute x8, starting transfers between devices, passed_along(): lax.ppermute(value, axis, [(source, source + steps) for source in range(f...  23 us
    max x27, other arithmetic, neighbour_step(): safe = jnp.maximum(column, 0)  18.8 us
    ge x27, other arithmetic, neighbour_step(): present = column >= 0  18.8 us
    another operation x1, loops' own time, near_field(): lax.scan(neighbour_step, start, (slot_ids.T, jnp.arange(27, dtype=jnp.int...  18.4 us
  transfers between devices with their start and end apart: 9, of which 2 were waited for; matrix products, arithmetic and copies ran while one was open for 77% of the time, Pallas kernels for 0%

profile of v1, /device:TPU:121, one launch (start us, length us, event | category | flops | bytes accessed | tf_op | source)
XLA Modules:
  0.0 834.7 jit_solution(15431301304054570373)
XLA Ops:
  81.6 10.0 %all-to-all-start = ((bf16[128,121,8]{1,2,0:T(8,128)(2,1)}), bf16[128,121,8]{1,2,0:T(8,128)(2,1)S(1)}, u32[]{:S(2)}, u32[]{:S(2)}) async-start(bf16[128,121,8]{1,2,0:T(8,128)(2,1)} %stack.8), calls=%async_computation | async-start | bytes 524288 | tf_op jit(solution)/shard_map/all_to_all | solution.py:142
  120.9 9.0 %collective-permute-done.7 = f32[16,4,128]{2,1,0:T(4,128)S(1)} collective-permute-done((f32[16,4,128]{2,1,0:T(4,128)S(1)}, f32[16,4,128]{2,1,0:T(4,128)S(1)}, u32[]{:S(2)}, u32[]{:S(2)}) %collective-permute-start.7) | collective-permute-done | bytes 32800 | tf_op jit(solution)/shard_map/ppermute | solution.py:19
  130.1 655.2 %while.13 = (s32[]{:T(128)}, f32[64,128]{1,0:T(8,128)S(1)}, f32[64,3,128]{2,1,0:T(4,128)S(1)}, s32[27,64]{1,0:T(8,128)}, f32[256,128]{1,0:T(8,128)S(1)}, /*index...) while((s32[]{:T(128)}, f32[64,128]{1,0:T(8,128)S(1)}, ...), condition=%wide.region_7.8_spmd.clone, body=%wide.region_3.7_spmd.clone.sunk | while | flops 24224900 | bytes 18192156 | solution.py:121
  131.4 6.0 fusion.453
  145.3 8.9 %fusion.455 = f32[64,3,128]{2,1,0:T(4,128)S(1)} fusion(f32[64,128,128]{2,1,0:T(8,128)} %get-tuple-element.385, f32[64,3,128]{2,1,0:T(4,128)S(1)} %gather_fusion, f32[64,3,128]{2,1,0:T(4,128)S(1)} %get-tuple-element.413), kind=kLoop, calls=%fused_computation.13.clone.1 | loop fusion | flops 9412608 | bytes 4489216 | tf_op jit(solution)/shard_map/while/body/eval_jaxpr/reduce_sum | solution.py:114
  155.7 6.0 fusion.453
  169.6 8.9 %fusion.455 = f32[64,3,128]{2,1,0:T(4,128)S(1)} fusion(f32[64,128,128]{2,1,0:T(8,128)} %get-tuple-element.385, f32[64,3,128]{2,1,0:T(4,128)S(1)} %gather_fusion, f32[64,3,128]{2,1,0:T(4,128)S(1)} %get-tuple-element.413), kind=kLoop, calls=%fused_computation.13.clone.1 | loop fusion | flops 9412608 | bytes 4489216 | tf_op jit(solution)/shard_map/while/body/eval_jaxpr/reduce_sum | solution.py:114
  180.0 6.0 fusion.453
  193.8 8.9 %fusion.455 = f32[64,3,128]{2,1,0:T(4,128)S(1)} fusion(f32[64,128,128]{2,1,0:T(8,128)} %get-tuple-element.385, f32[64,3,128]{2,1,0:T(4,128)S(1)} %gather_fusion, f32[64,3,128]{2,1,0:T(4,128)S(1)} %get-tuple-element.413), kind=kLoop, calls=%fused_computation.13.clone.1 | loop fusion | flops 9412608 | bytes 4489216 | tf_op jit(solution)/shard_map/while/body/eval_jaxpr/reduce_sum | solution.py:114
  204.2 6.0 fusion.453
  218.1 8.9 %fusion.455 = f32[64,3,128]{2,1,0:T(4,128)S(1)} fusion(f32[64,128,128]{2,1,0:T(8,128)} %get-tuple-element.385, f32[64,3,128]{2,1,0:T(4,128)S(1)} %gather_fusion, f32[64,3,128]{2,1,0:T(4,128)S(1)} %get-tuple-element.413), kind=kLoop, calls=%fused_computation.13.clone.1 | loop fusion | flops 9412608 | bytes 4489216 | tf_op jit(solution)/shard_map/while/body/eval_jaxpr/reduce_sum | solution.py:114
  228.5 6.0 fusion.453
  242.4 8.9 %fusion.455 = f32[64,3,128]{2,1,0:T(4,128)S(1)} fusion(f32[64,128,128]{2,1,0:T(8,128)} %get-tuple-element.385, f32[64,3,128]{2,1,0:T(4,128)S(1)} %gather_fusion, f32[64,3,128]{2,1,0:T(4,128)S(1)} %get-tuple-element.413), kind=kLoop, calls=%fused_computation.13.clone.1 | loop fusion | flops 9412608 | bytes 4489216 | tf_op jit(solution)/shard_map/while/body/eval_jaxpr/reduce_sum | solution.py:114
  252.8 6.0 fusion.453
  266.6 8.9 %fusion.455 = f32[64,3,128]{2,1,0:T(4,128)S(1)} fusion(f32[64,128,128]{2,1,0:T(8,128)} %get-tuple-element.385, f32[64,3,128]{2,1,0:T(4,128)S(1)} %gather_fusion, f32[64,3,128]{2,1,0:T(4,128)S(1)} %get-tuple-element.413), kind=kLoop, calls=%fused_computation.13.clone.1 | loop fusion | flops 9412608 | bytes 4489216 | tf_op jit(solution)/shard_map/while/body/eval_jaxpr/reduce_sum | solution.py:114
  277.0 6.0 fusion.453
  290.9 8.9 %fusion.455 = f32[64,3,128]{2,1,0:T(4,128)S(1)} fusion(f32[64,128,128]{2,1,0:T(8,128)} %get-tuple-element.385, f32[64,3,128]{2,1,0:T(4,128)S(1)} %gather_fusion, f32[64,3,128]{2,1,0:T(4,128)S(1)} %get-tuple-element.413), kind=kLoop, calls=%fused_computation.13.clone.1 | loop fusion | flops 9412608 | bytes 4489216 | tf_op jit(solution)/shard_map/while/body/eval_jaxpr/reduce_sum | solution.py:114
  301.3 6.0 fusion.453
  315.1 8.9 %fusion.455 = f32[64,3,128]{2,1,0:T(4,128)S(1)} fusion(f32[64,128,128]{2,1,0:T(8,128)} %get-tuple-element.385, f32[64,3,128]{2,1,0:T(4,128)S(1)} %gather_fusion, f32[64,3,128]{2,1,0:T(4,128)S(1)} %get-tuple-element.413), kind=kLoop, calls=%fused_computation.13.clone.1 | loop fusion | flops 9412608 | bytes 4489216 | tf_op jit(solution)/shard_map/while/body/eval_jaxpr/reduce_sum | solution.py:114
  325.5 6.0 fusion.453
  339.4 8.9 %fusion.455 = f32[64,3,128]{2,1,0:T(4,128)S(1)} fusion(f32[64,128,128]{2,1,0:T(8,128)} %get-tuple-element.385, f32[64,3,128]{2,1,0:T(4,128)S(1)} %gather_fusion, f32[64,3,128]{2,1,0:T(4,128)S(1)} %get-tuple-element.413), kind=kLoop, calls=%fused_computation.13.clone.1 | loop fusion | flops 9412608 | bytes 4489216 | tf_op jit(solution)/shard_map/while/body/eval_jaxpr/reduce_sum | solution.py:114
  349.8 6.0 fusion.453
  363.7 8.9 %fusion.455 = f32[64,3,128]{2,1,0:T(4,128)S(1)} fusion(f32[64,128,128]{2,1,0:T(8,128)} %get-tuple-element.385, f32[64,3,128]{2,1,0:T(4,128)S(1)} %gather_fusion, f32[64,3,128]{2,1,0:T(4,128)S(1)} %get-tuple-element.413), kind=kLoop, calls=%fused_computation.13.clone.1 | loop fusion | flops 9412608 | bytes 4489216 | tf_op jit(solution)/shard_map/while/body/eval_jaxpr/reduce_sum | solution.py:114
  374.1 6.0 fusion.453
  387.9 8.9 %fusion.455 = f32[64,3,128]{2,1,0:T(4,128)S(1)} fusion(f32[64,128,128]{2,1,0:T(8,128)} %get-tuple-element.385, f32[64,3,128]{2,1,0:T(4,128)S(1)} %gather_fusion, f32[64,3,128]{2,1,0:T(4,128)S(1)} %get-tuple-element.413), kind=kLoop, calls=%fused_computation.13.clone.1 | loop fusion | flops 9412608 | bytes 4489216 | tf_op jit(solution)/shard_map/while/body/eval_jaxpr/reduce_sum | solution.py:114
  398.3 6.0 fusion.453
  412.2 8.9 %fusion.455 = f32[64,3,128]{2,1,0:T(4,128)S(1)} fusion(f32[64,128,128]{2,1,0:T(8,128)} %get-tuple-element.385, f32[64,3,128]{2,1,0:T(4,128)S(1)} %gather_fusion, f32[64,3,128]{2,1,0:T(4,128)S(1)} %get-tuple-element.413), kind=kLoop, calls=%fused_computation.13.clone.1 | loop fusion | flops 9412608 | bytes 4489216 | tf_op jit(solution)/shard_map/while/body/eval_jaxpr/reduce_sum | solution.py:114
  422.6 6.0 fusion.453
  436.5 8.9 %fusion.455 = f32[64,3,128]{2,1,0:T(4,128)S(1)} fusion(f32[64,128,128]{2,1,0:T(8,128)} %get-tuple-element.385, f32[64,3,128]{2,1,0:T(4,128)S(1)} %gather_fusion, f32[64,3,128]{2,1,0:T(4,128)S(1)} %get-tuple-element.413), kind=kLoop, calls=%fused_computation.13.clone.1 | loop fusion | flops 9412608 | bytes 4489216 | tf_op jit(solution)/shard_map/while/body/eval_jaxpr/reduce_sum | solution.py:114
  446.9 6.0 fusion.453
  460.7 8.9 %fusion.455 = f32[64,3,128]{2,1,0:T(4,128)S(1)} fusion(f32[64,128,128]{2,1,0:T(8,128)} %get-tuple-element.385, f32[64,3,128]{2,1,0:T(4,128)S(1)} %gather_fusion, f32[64,3,128]{2,1,0:T(4,128)S(1)} %get-tuple-element.413), kind=kLoop, calls=%fused_computation.13.clone.1 | loop fusion | flops 9412608 | bytes 4489216 | tf_op jit(solution)/shard_map/while/body/eval_jaxpr/reduce_sum | solution.py:114
  471.1 6.0 fusion.453
  485.0 8.9 %fusion.455 = f32[64,3,128]{2,1,0:T(4,128)S(1)} fusion(f32[64,128,128]{2,1,0:T(8,128)} %get-tuple-element.385, f32[64,3,128]{2,1,0:T(4,128)S(1)} %gather_fusion, f32[64,3,128]{2,1,0:T(4,128)S(1)} %get-tuple-element.413), kind=kLoop, calls=%fused_computation.13.clone.1 | loop fusion | flops 9412608 | bytes 4489216 | tf_op jit(solution)/shard_map/while/body/eval_jaxpr/reduce_sum | solution.py:114
  495.4 6.0 fusion.453
  509.3 8.9 %fusion.455 = f32[64,3,128]{2,1,0:T(4,128)S(1)} fusion(f32[64,128,128]{2,1,0:T(8,128)} %get-tuple-element.385, f32[64,3,128]{2,1,0:T(4,128)S(1)} %gather_fusion, f32[64,3,128]{2,1,0:T(4,128)S(1)} %get-tuple-element.413), kind=kLoop, calls=%fused_computation.13.clone.1 | loop fusion | flops 9412608 | bytes 4489216 | tf_op jit(solution)/shard_map/while/body/eval_jaxpr/reduce_sum | solution.py:114
  533.5 8.9 %fusion.455 = f32[64,3,128]{2,1,0:T(4,128)S(1)} fusion(f32[64,128,128]{2,1,0:T(8,128)} %get-tuple-element.385, f32[64,3,128]{2,1,0:T(4,128)S(1)} %gather_fusion, f32[64,3,128]{2,1,0:T(4,128)S(1)} %get-tuple-element.413), kind=kLoop, calls=%fused_computation.13.clone.1 | loop fusion | flops 9412608 | bytes 4489216 | tf_op jit(solution)/shard_map/while/body/eval_jaxpr/reduce_sum | solution.py:114
  557.8 8.9 %fusion.455 = f32[64,3,128]{2,1,0:T(4,128)S(1)} fusion(f32[64,128,128]{2,1,0:T(8,128)} %get-tuple-element.385, f32[64,3,128]{2,1,0:T(4,128)S(1)} %gather_fusion, f32[64,3,128]{2,1,0:T(4,128)S(1)} %get-tuple-element.413), kind=kLoop, calls=%fused_computation.13.clone.1 | loop fusion | flops 9412608 | bytes 4489216 | tf_op jit(solution)/shard_map/while/body/eval_jaxpr/reduce_sum | solution.py:114
  582.1 8.9 %fusion.455 = f32[64,3,128]{2,1,0:T(4,128)S(1)} fusion(f32[64,128,128]{2,1,0:T(8,128)} %get-tuple-element.385, f32[64,3,128]{2,1,0:T(4,128)S(1)} %gather_fusion, f32[64,3,128]{2,1,0:T(4,128)S(1)} %get-tuple-element.413), kind=kLoop, calls=%fused_computation.13.clone.1 | loop fusion | flops 9412608 | bytes 4489216 | tf_op jit(solution)/shard_map/while/body/eval_jaxpr/reduce_sum | solution.py:114
  606.3 8.9 %fusion.455 = f32[64,3,128]{2,1,0:T(4,128)S(1)} fusion(f32[64,128,128]{2,1,0:T(8,128)} %get-tuple-element.385, f32[64,3,128]{2,1,0:T(4,128)S(1)} %gather_fusion, f32[64,3,128]{2,1,0:T(4,128)S(1)} %get-tuple-element.413), kind=kLoop, calls=%fused_computation.13.clone.1 | loop fusion | flops 9412608 | bytes 4489216 | tf_op jit(solution)/shard_map/while/body/eval_jaxpr/reduce_sum | solution.py:114
  630.6 8.9 %fusion.455 = f32[64,3,128]{2,1,0:T(4,128)S(1)} fusion(f32[64,128,128]{2,1,0:T(8,128)} %get-tuple-element.385, f32[64,3,128]{2,1,0:T(4,128)S(1)} %gather_fusion, f32[64,3,128]{2,1,0:T(4,128)S(1)} %get-tuple-element.413), kind=kLoop, calls=%fused_computation.13.clone.1 | loop fusion | flops 9412608 | bytes 4489216 | tf_op jit(solution)/shard_map/while/body/eval_jaxpr/reduce_sum | solution.py:114
  641.0 6.0 fusion.453
  654.9 8.9 %fusion.455 = f32[64,3,128]{2,1,0:T(4,128)S(1)} fusion(f32[64,128,128]{2,1,0:T(8,128)} %get-tuple-element.385, f32[64,3,128]{2,1,0:T(4,128)S(1)} %gather_fusion, f32[64,3,128]{2,1,0:T(4,128)S(1)} %get-tuple-element.413), kind=kLoop, calls=%fused_computation.13.clone.1 | loop fusion | flops 9412608 | bytes 4489216 | tf_op jit(solution)/shard_map/while/body/eval_jaxpr/reduce_sum | solution.py:114
  679.1 8.9 %fusion.455 = f32[64,3,128]{2,1,0:T(4,128)S(1)} fusion(f32[64,128,128]{2,1,0:T(8,128)} %get-tuple-element.385, f32[64,3,128]{2,1,0:T(4,128)S(1)} %gather_fusion, f32[64,3,128]{2,1,0:T(4,128)S(1)} %get-tuple-element.413), kind=kLoop, calls=%fused_computation.13.clone.1 | loop fusion | flops 9412608 | bytes 4489216 | tf_op jit(solution)/shard_map/while/body/eval_jaxpr/reduce_sum | solution.py:114
  689.5 6.0 fusion.453
  703.4 8.9 %fusion.455 = f32[64,3,128]{2,1,0:T(4,128)S(1)} fusion(f32[64,128,128]{2,1,0:T(8,128)} %get-tuple-element.385, f32[64,3,128]{2,1,0:T(4,128)S(1)} %gather_fusion, f32[64,3,128]{2,1,0:T(4,128)S(1)} %get-tuple-element.413), kind=kLoop, calls=%fused_computation.13.clone.1 | loop fusion | flops 9412608 | bytes 4489216 | tf_op jit(solution)/shard_map/while/body/eval_jaxpr/reduce_sum | solution.py:114
  727.7 8.9 %fusion.455 = f32[64,3,128]{2,1,0:T(4,128)S(1)} fusion(f32[64,128,128]{2,1,0:T(8,128)} %get-tuple-element.385, f32[64,3,128]{2,1,0:T(4,128)S(1)} %gather_fusion, f32[64,3,128]{2,1,0:T(4,128)S(1)} %get-tuple-element.413), kind=kLoop, calls=%fused_computation.13.clone.1 | loop fusion | flops 9412608 | bytes 4489216 | tf_op jit(solution)/shard_map/while/body/eval_jaxpr/reduce_sum | solution.py:114
  751.9 8.9 %fusion.455 = f32[64,3,128]{2,1,0:T(4,128)S(1)} fusion(f32[64,128,128]{2,1,0:T(8,128)} %get-tuple-element.385, f32[64,3,128]{2,1,0:T(4,128)S(1)} %gather_fusion, f32[64,3,128]{2,1,0:T(4,128)S(1)} %get-tuple-element.413), kind=kLoop, calls=%fused_computation.13.clone.1 | loop fusion | flops 9412608 | bytes 4489216 | tf_op jit(solution)/shard_map/while/body/eval_jaxpr/reduce_sum | solution.py:114
  776.2 8.9 %fusion.455 = f32[64,3,128]{2,1,0:T(4,128)S(1)} fusion(f32[64,128,128]{2,1,0:T(8,128)} %get-tuple-element.385, f32[64,3,128]{2,1,0:T(4,128)S(1)} %gather_fusion, f32[64,3,128]{2,1,0:T(4,128)S(1)} %get-tuple-element.413), kind=kLoop, calls=%fused_computation.13.clone.1 | loop fusion | flops 9412608 | bytes 4489216 | tf_op jit(solution)/shard_map/while/body/eval_jaxpr/reduce_sum | solution.py:114
  (858 shorter events, 447.6 us)
Async XLA Ops:
  40.9 36.7 %copy-start.1 = (f32[64,128]{1,0:T(8,128)S(1)}, f32[64,128]{1,0:T(8,128)}, u32[]{:S(2)}) copy-start(f32[64,128]{1,0:T(8,128)} %param.11) | copy-start | bytes 98308
  64.2 27.5 %copy-start.4 = (s32[1,2,32]{2,1,0:T(2,128)S(1)}, s32[1,2,32]{2,1,0:T(2,128)}, u32[]{:S(2)}) copy-start(s32[1,2,32]{2,1,0:T(2,128)} %param.12) | copy-start | bytes 772
  65.5 26.9 %copy-start = (f32[64,3,128]{2,0,1:T(8,128)S(1)}, f32[64,3,128]{2,0,1:T(8,128)}, u32[]{:S(2)}) copy-start(f32[64,3,128]{2,0,1:T(8,128)} %param.10) | copy-start | bytes 294916
  74.4 23.4 %copy-start.5 = (s32[1,2,32]{2,1,0:T(2,128)S(1)}, s32[1,2,32]{2,1,0:T(2,128)}, u32[]{:S(2)}) copy-start(s32[1,2,32]{2,1,0:T(2,128)} %param.13) | copy-start | bytes 772
  74.4 23.5 %copy-start.3 = (s32[1,4,16]{2,1,0:T(4,128)S(1)}, s32[1,4,16]{2,1,0:T(4,128)}, u32[]{:S(2)}) copy-start(s32[1,4,16]{2,1,0:T(4,128)} %param.14) | copy-start | bytes 772
  80.8 28.9 %copy-start.2 = (s32[8,316]{1,0:T(8,128)S(1)}, s32[8,316]{1,0:T(8,128)}, u32[]{:S(2)}) copy-start(s32[8,316]{1,0:T(8,128)} %param.16) | copy-start | bytes 30340
  81.6 703.6 %all-to-all-start = ((bf16[128,121,8]{1,2,0:T(8,128)(2,1)}), bf16[128,121,8]{1,2,0:T(8,128)(2,1)S(1)}, u32[]{:S(2)}, u32[]{:S(2)}) async-start(bf16[128,121,8]{1,2,0:T(8,128)(2,1)} %stack.8), calls=%async_computation | async-start | bytes 524288 | tf_op jit(solution)/shard_map/all_to_all | solution.py:142
  93.5 16.5 %collective-permute-start = (f32[32,4,128]{2,1,0:T(4,128)S(1)}, f32[32,4,128]{2,1,0:T(4,128)S(1)}, u32[]{:S(2)}, u32[]{:S(2)}) collective-permute-start(f32[32,4,128]{2,1,0:T(4,128)S(1)} %get-tuple-element.310), channel_id=1, source_target_pairs={{0,32},{32,64},{64,96},{1,33},{33,65},{65,97},{2,34},{34,66},{66,9... | collective-permute-start | bytes 196616 | tf_op jit(solution)/shard_map/ppermute | solution.py:19
  96.6 17.5 %collective-permute-start.1 = (f32[32,4,128]{2,1,0:T(4,128)S(1)}, f32[32,4,128]{2,1,0:T(4,128)S(1)}, u32[]{:S(2)}, u32[]{:S(2)}) collective-permute-start(f32[32,4,128]{2,1,0:T(4,128)S(1)} %get-tuple-element.309), channel_id=1, source_target_pairs={{32,0},{64,32},{96,64},{33,1},{65,33},{97,65},{34,2},{66,34},{98,6... | collective-permute-start | bytes 196616 | tf_op jit(solution)/shard_map/ppermute | solution.py:19
  99.8 19.2 %collective-permute-start.2 = (f32[32,4,128]{2,1,0:T(4,128)S(1)}, f32[32,4,128]{2,1,0:T(4,128)S(1)}, u32[]{:S(2)}, u32[]{:S(2)}) collective-permute-start(f32[32,4,128]{2,1,0:T(4,128)S(1)} %get-tuple-element.308), channel_id=1, source_target_pairs={{0,1},{1,2},{2,3},{3,4},{4,5},{5,6},{6,7},{7,8},{8,9},{9,10},{10,1... | collective-permute-start | bytes 196616 | tf_op jit(solution)/shard_map/ppermute | solution.py:19
  101.1 19.4 %collective-permute-start.3 = (f32[32,4,128]{2,1,0:T(4,128)S(1)}, f32[32,4,128]{2,1,0:T(4,128)S(1)}, u32[]{:S(2)}, u32[]{:S(2)}) collective-permute-start(f32[32,4,128]{2,1,0:T(4,128)S(1)} %get-tuple-element.307), channel_id=1, source_target_pairs={{1,0},{2,1},{3,2},{4,3},{5,4},{6,5},{7,6},{8,7},{9,8},{10,9},{11,1... | collective-permute-start | bytes 196616 | tf_op jit(solution)/shard_map/ppermute | solution.py:19
  105.9 14.6 %collective-permute-start.4 = (f32[16,4,128]{2,1,0:T(4,128)S(1)}, f32[16,4,128]{2,1,0:T(4,128)S(1)}, u32[]{:S(2)}, u32[]{:S(2)}) collective-permute-start(f32[16,4,128]{2,1,0:T(4,128)S(1)} %get-tuple-element.304), channel_id=1, source_target_pairs={{0,33},{1,34},{2,35},{3,36},{4,37},{5,38},{6,39},{7,40},{8,41},{9,... | collective-permute-start | bytes 98312 | tf_op jit(solution)/shard_map/ppermute | solution.py:19
  110.0 10.5 %collective-permute-start.5 = (f32[16,4,128]{2,1,0:T(4,128)S(1)}, f32[16,4,128]{2,1,0:T(4,128)S(1)}, u32[]{:S(2)}, u32[]{:S(2)}) collective-permute-start(f32[16,4,128]{2,1,0:T(4,128)S(1)} %get-tuple-element.305), channel_id=1, source_target_pairs={{0,31},{1,32},{2,33},{3,34},{4,35},{5,36},{6,37},{7,38},{8,39},{9,... | collective-permute-start | bytes 98312 | tf_op jit(solution)/shard_map/ppermute | solution.py:19
  114.1 6.8 collective-permute-start.6
  118.9 11.0 %collective-permute-start.7 = (f32[16,4,128]{2,1,0:T(4,128)S(1)}, f32[16,4,128]{2,1,0:T(4,128)S(1)}, u32[]{:S(2)}, u32[]{:S(2)}) collective-permute-start(f32[16,4,128]{2,1,0:T(4,128)S(1)} %get-tuple-element.303), channel_id=1, source_target_pairs={{33,0},{34,1},{35,2},{36,3},{37,4},{38,5},{39,6},{40,7},{41,8},{42... | collective-permute-start | bytes 98312 | tf_op jit(solution)/shard_map/ppermute | solution.py:19
